TPU v7x, 32 devices: a whole 2x2x4 slice. The times are simulated.
32 devices in a mesh: rep: 2 (over y), seq: 4 (over x, core), head: 4 (over z).
Axes of the slice: x: 2, y: 2, z: 4, core: 2. Of those that a mesh axis runs over, the one named last changes fastest.
Arguments:
- queries: bfloat16 [2048, 4096], P(('rep', 'seq', 'head')), parts along dimension 0, may hold values from -6 to 6
- key_rows: bfloat16 [2048, 4096], P(('rep', 'seq', 'head')), parts along dimension 0, may hold values from -6 to 6
- value_rows: bfloat16 [2048, 4096], P(('rep', 'seq', 'head')), parts along dimension 0, may hold values from -6 to 6
- out_grad: bfloat16 [2048, 4096], P(('rep', 'seq', 'head')), parts along dimension 0, may hold values from -6 to 6
Outputs:
- attended: bfloat16 [2048, 4096], P(('rep', 'seq', 'head')), parts along dimension 0
- query_grad: bfloat16 [2048, 4096], P(('rep', 'seq', 'head')), parts along dimension 0
- key_grad: bfloat16 [2048, 4096], P(('rep', 'seq', 'head')), parts along dimension 0
- value_grad: bfloat16 [2048, 4096], P(('rep', 'seq', 'head')), parts along dimension 0
There are 2 independent parts, one for each index of `rep`. A program takes and returns all parts, laid end to end along the dimension named above; each array names one. Nothing has to cross between parts.
All inputs are finite; a program needn't handle non-finite values.
Results may differ from a plain program's by a relative error of at most 0.0049.
Values may be sent and summed in bfloat16 or wider, within the bound.
A program may use at most 64 MiB of HBM per device.

v0:
```python
import jax
import jax.numpy as jnp
from jax import lax
from jax.sharding import PartitionSpec as P

DH = 128
BLK_MAX = 512


def shards(queries, key_rows, value_rows, out_grad):
    f32 = jnp.float32
    bf16 = jnp.bfloat16
    head_count = lax.axis_size("head")
    tok_count = queries.shape[0]
    local_heads = queries.shape[1] // (head_count * DH)
    seq_rows = tok_count * head_count
    block = min(BLK_MAX, seq_rows)
    block_count = seq_rows // block
    factor = float(DH * seq_rows * lax.axis_size("seq")) ** (-0.5)

    def to_heads(matrix):
        return matrix.reshape(tok_count, head_count, local_heads, DH)

    def per_head(parts):
        heads_here = parts[0].shape[2]
        query_blocks, key_blocks, value_blocks, grad_blocks = (
            item.reshape(block_count, block, heads_here, DH) for item in parts
        )
        kv_state = jnp.einsum(
            "bthd,bthe->bhde", key_blocks, value_blocks, preferred_element_type=f32
        )
        grad_state = jnp.einsum(
            "bthd,bthe->bhde", query_blocks, grad_blocks, preferred_element_type=f32
        )
        empty_state = jnp.zeros((1, heads_here, DH, DH), f32)
        local_prefix = jnp.concatenate([empty_state, jnp.cumsum(kv_state, 0)[:-1]], 0)
        tail_sums = jnp.cumsum(grad_state[::-1], 0)[::-1]
        local_suffix = jnp.concatenate([tail_sums[1:], empty_state], 0)
        kv_total = jnp.sum(kv_state, 0)
        grad_total = jnp.sum(grad_state, 0)
        my_index = lax.axis_index("seq")
        pieces = (
            lax.all_gather(kv_total[None], "seq", axis=0, tiled=True),
            lax.all_gather(grad_total[None], "seq", axis=0, tiled=True),
        )
        count = pieces[0].shape[0]
        index = jnp.arange(count, dtype=jnp.int32)
        below_me = (index < my_index).astype(f32)[:, None, None, None]
        above_me = (index > my_index).astype(f32)[:, None, None, None]
        span_prefix = jnp.sum(pieces[0] * below_me, 0)
        span_suffix = jnp.sum(pieces[1] * above_me, 0)
        prefix = (local_prefix + span_prefix[None]).astype(bf16)
        suffix = (local_suffix + span_suffix[None]).astype(bf16)
        causal = (jnp.arange(block)[:, None] >= jnp.arange(block)[None, :])[None, None]
        scores = jnp.einsum("bthd,bshd->bhts", query_blocks, key_blocks, preferred_element_type=f32)
        scores = jnp.where(causal, scores * factor, 0.0).astype(bf16)
        attended = jnp.einsum("bhts,bshd->bthd", scores, value_blocks, preferred_element_type=f32)
        attended = attended + factor * jnp.einsum(
            "bthd,bhde->bthe", query_blocks, prefix, preferred_element_type=f32
        )
        dscores = jnp.einsum(
            "bthe,bshe->bhts", grad_blocks, value_blocks, preferred_element_type=f32
        )
        dscores = jnp.where(causal, dscores * factor, 0.0).astype(bf16)
        query_grad = jnp.einsum("bhts,bshd->bthd", dscores, key_blocks, preferred_element_type=f32)
        query_grad = query_grad + factor * jnp.einsum(
            "bthe,bhde->bthd", grad_blocks, prefix, preferred_element_type=f32
        )
        key_grad = jnp.einsum("bhts,bthd->bshd", dscores, query_blocks, preferred_element_type=f32)
        key_grad = key_grad + factor * jnp.einsum(
            "bshe,bhde->bshd", value_blocks, suffix, preferred_element_type=f32
        )
        value_grad = jnp.einsum("bhts,bthe->bshe", scores, grad_blocks, preferred_element_type=f32)
        value_grad = value_grad + factor * jnp.einsum(
            "bshd,bhde->bshe", key_blocks, suffix, preferred_element_type=f32
        )
        results = tuple(
            (
                item.astype(bf16).reshape(seq_rows, 1, heads_here, DH)
                for item in (attended, query_grad, key_grad, value_grad)
            )
        )
        return (
            lax.all_to_all(results[0], "head", split_axis=0, concat_axis=1, tiled=True),
            lax.all_to_all(results[1], "head", split_axis=0, concat_axis=1, tiled=True),
            lax.all_to_all(results[2], "head", split_axis=0, concat_axis=1, tiled=True),
            lax.all_to_all(results[3], "head", split_axis=0, concat_axis=1, tiled=True),
        )

    outputs = per_head(
        (
            lax.all_to_all(to_heads(queries), "head", split_axis=1, concat_axis=0, tiled=True),
            lax.all_to_all(to_heads(key_rows), "head", split_axis=1, concat_axis=0, tiled=True),
            lax.all_to_all(to_heads(value_rows), "head", split_axis=1, concat_axis=0, tiled=True),
            lax.all_to_all(to_heads(out_grad), "head", split_axis=1, concat_axis=0, tiled=True),
        )
    )
    return tuple((item.reshape(tok_count, queries.shape[1]) for item in outputs))


def solution(mesh):
    placed = (
        P(("rep", "seq", "head"), None),
        P(("rep", "seq", "head"), None),
        P(("rep", "seq", "head"), None),
        P(("rep", "seq", "head"), None),
    )
    return jax.shard_map(
        shards,
        mesh=mesh,
        in_specs=placed,
        out_specs=(
            P(("rep", "seq", "head"), None),
            P(("rep", "seq", "head"), None),
            P(("rep", "seq", "head"), None),
            P(("rep", "seq", "head"), None),
        ),
        check_vma=False,
    )
```

profile of v0, /device:TPU:0, one launch (start us, length us, event | category | flops | bytes accessed | tf_op | source)
XLA Modules:
  0.0 174.0 jit_solution(1147366358603336593)
XLA Ops:
  7.2 1.2 copy.85
  9.4 6.3 %all-to-all-start.1 = ((bf16[64,4,8,128]{3,0,2,1:T(8,128)(2,1)}), bf16[64,4,8,128]{3,0,2,1:T(8,128)(2,1)S(1)}, u32[]{:S(2)}, u32[]{:S(2)}) async-start(bf16[64,4,8,128]{3,0,2,1:T(8,128)(2,1)} %copy.50), calls=%async_computation.1 | async-start | bytes 1048576 | tf_op jit(solution)/shard_map/all_to_all | solution.py:93
  16.8 13.4 %all-to-all-done.1 = bf16[64,4,8,128]{3,0,2,1:T(8,128)(2,1)S(1)} async-done(((bf16[64,4,8,128]{3,0,2,1:T(8,128)(2,1)}), bf16[64,4,8,128]{3,0,2,1:T(8,128)(2,1)S(1)}, u32[]{:S(2)}, u32[]{:S(2)}) %all-to-all-start.1) | async-done | bytes 524320 | tf_op jit(solution)/shard_map/all_to_all | solution.py:93
  30.2 3.5 %all-to-all-start.2 = ((bf16[64,4,8,128]{3,0,2,1:T(8,128)(2,1)}), bf16[64,4,8,128]{3,0,2,1:T(8,128)(2,1)S(1)}, u32[]{:S(2)}, u32[]{:S(2)}) async-start(bf16[64,4,8,128]{3,0,2,1:T(8,128)(2,1)} %copy.52), calls=%async_computation.2 | async-start | bytes 1048576 | tf_op jit(solution)/shard_map/all_to_all | solution.py:94
  33.8 13.9 %all-to-all-done.2 = bf16[64,4,8,128]{3,0,2,1:T(8,128)(2,1)S(1)} async-done(((bf16[64,4,8,128]{3,0,2,1:T(8,128)(2,1)}), bf16[64,4,8,128]{3,0,2,1:T(8,128)(2,1)S(1)}, u32[]{:S(2)}, u32[]{:S(2)}) %all-to-all-start.2) | async-done | bytes 524320 | tf_op jit(solution)/shard_map/all_to_all | solution.py:94
  47.7 1.1 fusion.16
  49.9 3.5 %all-to-all-start = ((bf16[64,4,8,128]{3,0,2,1:T(8,128)(2,1)}), bf16[64,4,8,128]{3,0,2,1:T(8,128)(2,1)S(1)}, u32[]{:S(2)}, u32[]{:S(2)}) async-start(bf16[64,4,8,128]{3,0,2,1:T(8,128)(2,1)} %copy.48), calls=%async_computation | async-start | bytes 1048576 | tf_op jit(solution)/shard_map/all_to_all | solution.py:92
  54.5 12.8 %all-to-all-done = bf16[64,4,8,128]{3,0,2,1:T(8,128)(2,1)S(1)} async-done(((bf16[64,4,8,128]{3,0,2,1:T(8,128)(2,1)}), bf16[64,4,8,128]{3,0,2,1:T(8,128)(2,1)S(1)}, u32[]{:S(2)}, u32[]{:S(2)}) %all-to-all-start) | async-done | bytes 524320 | tf_op jit(solution)/shard_map/all_to_all | solution.py:92
  67.4 3.5 %all-to-all-start.4 = ((bf16[64,4,8,128]{3,0,2,1:T(8,128)(2,1)}), bf16[64,4,8,128]{3,0,2,1:T(8,128)(2,1)S(1)}, u32[]{:S(2)}, u32[]{:S(2)}) async-start(bf16[64,4,8,128]{3,0,2,1:T(8,128)(2,1)} %copy.59), calls=%async_computation.4 | async-start | bytes 1048576 | tf_op jit(solution)/shard_map/all_to_all | solution.py:95
  70.9 13.9 %all-to-all-done.4 = bf16[64,4,8,128]{3,0,2,1:T(8,128)(2,1)S(1)} async-done(((bf16[64,4,8,128]{3,0,2,1:T(8,128)(2,1)}), bf16[64,4,8,128]{3,0,2,1:T(8,128)(2,1)S(1)}, u32[]{:S(2)}, u32[]{:S(2)}) %all-to-all-start.4) | async-done | bytes 524320 | tf_op jit(solution)/shard_map/all_to_all | solution.py:95
  84.8 1.1 fusion.17
  86.5 1.4 convolution_bitcast_fusion.3
  87.9 1.9 %multiply_reduce_fusion.1 = bf16[8,128,128]{2,1,0:T(8,128)(2,1)S(1)} fusion(f32[4,8,128,128]{3,2,1,0:T(8,128)} %bitcast.130, f32[4]{0:T(128)S(1)} %compare_convert_fusion.1), kind=kLoop, calls=%fused_computation.2 | loop fusion | flops 917504 | bytes 2359312 | tf_op jit(solution)/shard_map/reduce_sum | solution.py:50
  90.2 1.1 copy.57
  91.3 4.1 %all-to-all-start.3 = ((bf16[256,1,8,128]{3,2,1,0:T(8,128)(2,1)}), bf16[256,1,8,128]{3,2,1,0:T(8,128)(2,1)}, u32[]{:S(2)}, u32[]{:S(2)}) async-start(bf16[256,1,8,128]{3,2,1,0:T(8,128)(2,1)} %copy.57), calls=%async_computation.3 | async-start | bytes 1048576 | tf_op jit(solution)/shard_map/all_to_all | solution.py:84
  95.5 1.5 convolution_bitcast_fusion
  96.9 10.9 %all-gather.7.cloned.1.call-done = f32[32,128,128]{2,1,0:T(8,128)} async-done(((f32[8,128,128]{2,1,0:T(8,128)}), f32[32,128,128]{2,1,0:T(8,128)}) %all-gather.7.cloned.1.call-update) | async-done | bytes 2097168 | tf_op jit(solution)/shard_map/all_gather | solution.py:44
  107.9 1.9 %multiply_reduce_fusion = bf16[8,128,128]{2,1,0:T(8,128)(2,1)S(1)} fusion(f32[4,8,128,128]{3,2,1,0:T(8,128)} %bitcast.131, f32[4]{0:T(128)S(1)} %compare_convert_fusion), kind=kLoop, calls=%fused_computation | loop fusion | flops 917504 | bytes 2359312 | tf_op jit(solution)/shard_map/reduce_sum | solution.py:51
  111.6 4.6 %all-to-all-start.7 = ((bf16[256,1,8,128]{3,2,1,0:T(8,128)(2,1)}), bf16[256,1,8,128]{3,2,1,0:T(8,128)(2,1)}, u32[]{:S(2)}, u32[]{:S(2)}) async-start(bf16[256,1,8,128]{3,2,1,0:T(8,128)(2,1)} %copy.72), calls=%async_computation.7 | async-start | bytes 1048576 | tf_op jit(solution)/shard_map/all_to_all | solution.py:87
  118.6 12.6 %all-to-all-done.7 = bf16[256,1,8,128]{3,2,1,0:T(8,128)(2,1)} async-done(((bf16[256,1,8,128]{3,2,1,0:T(8,128)(2,1)}), bf16[256,1,8,128]{3,2,1,0:T(8,128)(2,1)}, u32[]{:S(2)}, u32[]{:S(2)}) %all-to-all-start.7) | async-done | bytes 524320 | tf_op jit(solution)/shard_map/all_to_all | solution.py:87
  131.2 3.5 %all-to-all-start.6 = ((bf16[256,1,8,128]{3,2,1,0:T(8,128)(2,1)}), bf16[256,1,8,128]{3,2,1,0:T(8,128)(2,1)S(1)}, u32[]{:S(2)}, u32[]{:S(2)}) async-start(bf16[256,1,8,128]{3,2,1,0:T(8,128)(2,1)} %copy.67), calls=%async_computation.6 | async-start | bytes 1048576 | tf_op jit(solution)/shard_map/all_to_all | solution.py:86
  136.5 12.1 %all-to-all-done.6 = bf16[256,1,8,128]{3,2,1,0:T(8,128)(2,1)S(1)} async-done(((bf16[256,1,8,128]{3,2,1,0:T(8,128)(2,1)}), bf16[256,1,8,128]{3,2,1,0:T(8,128)(2,1)S(1)}, u32[]{:S(2)}, u32[]{:S(2)}) %all-to-all-start.6) | async-done | bytes 524320 | tf_op jit(solution)/shard_map/all_to_all | solution.py:86
  148.7 3.5 %all-to-all-start.5 = ((bf16[256,1,8,128]{3,2,1,0:T(8,128)(2,1)}), bf16[256,1,8,128]{3,2,1,0:T(8,128)(2,1)S(1)}, u32[]{:S(2)}, u32[]{:S(2)}) async-start(bf16[256,1,8,128]{3,2,1,0:T(8,128)(2,1)} %copy.62), calls=%async_computation.5 | async-start | bytes 1048576 | tf_op jit(solution)/shard_map/all_to_all | solution.py:85
  157.6 8.5 %all-to-all-done.5 = bf16[256,1,8,128]{3,2,1,0:T(8,128)(2,1)S(1)} async-done(((bf16[256,1,8,128]{3,2,1,0:T(8,128)(2,1)}), bf16[256,1,8,128]{3,2,1,0:T(8,128)(2,1)S(1)}, u32[]{:S(2)}, u32[]{:S(2)}) %all-to-all-start.5) | async-done | bytes 524320 | tf_op jit(solution)/shard_map/all_to_all | solution.py:85
  (53 shorter events, 17.9 us)
Async XLA Ops:
  7.2 8.5 %copy-start.4 = (bf16[64,4096]{1,0:T(8,128)(2,1)S(1)}, bf16[64,4096]{1,0:T(8,128)(2,1)}, u32[]{:S(2)}) copy-start(bf16[64,4096]{1,0:T(8,128)(2,1)} %param.6) | copy-start | bytes 1572868
  9.4 20.8 %all-to-all-start.1 = ((bf16[64,4,8,128]{3,0,2,1:T(8,128)(2,1)}), bf16[64,4,8,128]{3,0,2,1:T(8,128)(2,1)S(1)}, u32[]{:S(2)}, u32[]{:S(2)}) async-start(bf16[64,4,8,128]{3,0,2,1:T(8,128)(2,1)} %copy.50), calls=%async_computation.1 | async-start | bytes 1048576 | tf_op jit(solution)/shard_map/all_to_all | solution.py:93
  30.2 17.4 %all-to-all-start.2 = ((bf16[64,4,8,128]{3,0,2,1:T(8,128)(2,1)}), bf16[64,4,8,128]{3,0,2,1:T(8,128)(2,1)S(1)}, u32[]{:S(2)}, u32[]{:S(2)}) async-start(bf16[64,4,8,128]{3,0,2,1:T(8,128)(2,1)} %copy.52), calls=%async_computation.2 | async-start | bytes 1048576 | tf_op jit(solution)/shard_map/all_to_all | solution.py:94
  33.7 54.2 %all-gather.5.cloned.1.call-start = ((), (), s32[]{:S(2)}) async-start(), calls=%async_computation.8 | async-start | bytes 2621440 | tf_op jit(solution)/shard_map/all_gather | solution.py:43
  33.7 15.1 %copy-start.5 = (bf16[64,4096]{1,0:T(8,128)(2,1)S(1)}, bf16[64,4096]{1,0:T(8,128)(2,1)}, u32[]{:S(2)}) copy-start(bf16[64,4096]{1,0:T(8,128)(2,1)} %param.4) | copy-start | bytes 1572868
  48.8 4.6 %copy-start.6 = (bf16[64,4096]{1,0:T(8,128)(2,1)S(1)}, bf16[64,4096]{1,0:T(8,128)(2,1)}, u32[]{:S(2)}) copy-start(bf16[64,4096]{1,0:T(8,128)(2,1)} %param.7) | copy-start | bytes 1572868
  49.9 17.4 %all-to-all-start = ((bf16[64,4,8,128]{3,0,2,1:T(8,128)(2,1)}), bf16[64,4,8,128]{3,0,2,1:T(8,128)(2,1)S(1)}, u32[]{:S(2)}, u32[]{:S(2)}) async-start(bf16[64,4,8,128]{3,0,2,1:T(8,128)(2,1)} %copy.48), calls=%async_computation | async-start | bytes 1048576 | tf_op jit(solution)/shard_map/all_to_all | solution.py:92
  67.4 17.4 %all-to-all-start.4 = ((bf16[64,4,8,128]{3,0,2,1:T(8,128)(2,1)}), bf16[64,4,8,128]{3,0,2,1:T(8,128)(2,1)S(1)}, u32[]{:S(2)}, u32[]{:S(2)}) async-start(bf16[64,4,8,128]{3,0,2,1:T(8,128)(2,1)} %copy.59), calls=%async_computation.4 | async-start | bytes 1048576 | tf_op jit(solution)/shard_map/all_to_all | solution.py:95
  70.8 37.0 %all-gather.7.cloned.1.call-start = ((), (), s32[]{:S(2)}) async-start(), calls=%async_computation.9 | async-start | bytes 2621440 | tf_op jit(solution)/shard_map/all_gather | solution.py:44
  87.9 1.9 %copy-start.1 = (f32[8,128,256]{1,2,0:T(8,128)S(1)}, f32[8,128,256]{1,2,0:T(8,128)}, u32[]{:S(2)}) copy-start(f32[8,128,256]{1,2,0:T(8,128)} %convolution_bitcast_fusion.3) | copy-start | bytes 3145732
  91.3 20.3 %all-to-all-start.3 = ((bf16[256,1,8,128]{3,2,1,0:T(8,128)(2,1)}), bf16[256,1,8,128]{3,2,1,0:T(8,128)(2,1)}, u32[]{:S(2)}, u32[]{:S(2)}) async-start(bf16[256,1,8,128]{3,2,1,0:T(8,128)(2,1)} %copy.57), calls=%async_computation.3 | async-start | bytes 1048576 | tf_op jit(solution)/shard_map/all_to_all | solution.py:84
  96.9 12.8 %copy-start = (f32[8,128,256]{1,2,0:T(8,128)S(1)}, f32[8,128,256]{1,2,0:T(8,128)}, u32[]{:S(2)}) copy-start(f32[8,128,256]{1,2,0:T(8,128)} %convolution_bitcast_fusion) | copy-start | bytes 3145732
  109.7 0.7 copy-start.2
  111.6 19.6 %all-to-all-start.7 = ((bf16[256,1,8,128]{3,2,1,0:T(8,128)(2,1)}), bf16[256,1,8,128]{3,2,1,0:T(8,128)(2,1)}, u32[]{:S(2)}, u32[]{:S(2)}) async-start(bf16[256,1,8,128]{3,2,1,0:T(8,128)(2,1)} %copy.72), calls=%async_computation.7 | async-start | bytes 1048576 | tf_op jit(solution)/shard_map/all_to_all | solution.py:87
  116.2 0.9 copy-start.3
  131.2 17.5 %all-to-all-start.6 = ((bf16[256,1,8,128]{3,2,1,0:T(8,128)(2,1)}), bf16[256,1,8,128]{3,2,1,0:T(8,128)(2,1)S(1)}, u32[]{:S(2)}, u32[]{:S(2)}) async-start(bf16[256,1,8,128]{3,2,1,0:T(8,128)(2,1)} %copy.67), calls=%async_computation.6 | async-start | bytes 1048576 | tf_op jit(solution)/shard_map/all_to_all | solution.py:86
  148.7 17.4 %all-to-all-start.5 = ((bf16[256,1,8,128]{3,2,1,0:T(8,128)(2,1)}), bf16[256,1,8,128]{3,2,1,0:T(8,128)(2,1)S(1)}, u32[]{:S(2)}, u32[]{:S(2)}) async-start(bf16[256,1,8,128]{3,2,1,0:T(8,128)(2,1)} %copy.62), calls=%async_computation.5 | async-start | bytes 1048576 | tf_op jit(solution)/shard_map/all_to_all | solution.py:85
Sparse Core Ops, SparseCore 0:
  49.0 21.6 all-gather.4
  86.1 21.6 all-gather.6
where the time goes:
time: 175 us; the launch traced here: 174 us
  waiting for transfers between devices  98.2 us (56%)
  starting transfers between devices  32.5 us (19%)
  local copies, waits for them, and re-layouts  17.1 us (10%)
  between operations  14.3 us (8%)
  matrix products  8.12 us (5%)
  other arithmetic  3.83 us (2%)
    all_to_all x1, waiting for transfers between devices, shards(): lax.all_to_all(to_heads(value_rows), 'head', split_axis=1, concat_axis=0,...  13.9 us
    all_to_all x1, waiting for transfers between devices, shards(): lax.all_to_all(to_heads(out_grad), 'head', split_axis=1, concat_axis=0, t...  13.9 us
    all_to_all x1, waiting for transfers between devices, shards(): lax.all_to_all(to_heads(key_rows), 'head', split_axis=1, concat_axis=0, t...  13.4 us
    all_to_all x1, waiting for transfers between devices, shards(): lax.all_to_all(to_heads(queries), 'head', split_axis=1, concat_axis=0, ti...  12.8 us
    all_to_all x1, waiting for transfers between devices, per_head(): lax.all_to_all(results[3], 'head', split_axis=0, concat_axis=1, tiled=True)  12.6 us
    all_to_all x1, waiting for transfers between devices, per_head(): lax.all_to_all(results[2], 'head', split_axis=0, concat_axis=1, tiled=True)  12.1 us
    all_gather x1, waiting for transfers between devices, per_head(): lax.all_gather(grad_total[None], 'seq', axis=0, tiled=True)  10.9 us
    all_to_all x1, waiting for transfers between devices, per_head(): lax.all_to_all(results[1], 'head', split_axis=0, concat_axis=1, tiled=True)  8.53 us
  transfers between devices with their start and end apart: 10, of which 8 were waited for; matrix products, arithmetic and copies ran while one was open for 14% of the time, Pallas kernels for 0%

commit v1 on v0

--- a/solution.py
+++ b/solution.py
@@ -5,6 +5,20 @@
 
 DH = 128
 BLK_MAX = 512
+
+
+def create_routes_all(m, dim_no, frame):
+    wide_out = m.shape
+    v_now = m.reshape(*wide_out[:dim_no], frame, wide_out[dim_no] // frame, *wide_out[dim_no + 1 :])
+    a_next = jnp.moveaxis(v_now, dim_no, 0)
+    return a_next
+
+
+def shifts_all_remake(inner_x, array_dim):
+    extra = list(inner_x.shape[1:])
+    extra[array_dim] *= inner_x.shape[0]
+    step_out = jnp.moveaxis(inner_x, 0, array_dim).reshape(extra)
+    return step_out
 
 
 def shards(queries, key_rows, value_rows, out_grad):
@@ -87,10 +101,27 @@
             lax.all_to_all(results[3], "head", split_axis=0, concat_axis=1, tiled=True),
         )
 
+    def draw_quarters(local_x, net_axis, original, q_in):
+        p_next = jax.lax.axis_size(net_axis)
+        state_next = jax.lax.axis_index(net_axis)
+        block_last, seen_now = (p_next, state_next)
+        lower = create_routes_all(local_x, original, block_last)
+        shelf = [lower[seen_now]]
+        ii = 1
+        while ii < block_last:
+            w2 = lower[seen_now ^ ii]
+            oldest = jax.lax.ppermute(w2, net_axis, [(q, q ^ ii) for q in range(block_last)])
+            shelf.append(oldest)
+            ii += 1
+        outer = jnp.stack(shelf)
+        lower = outer[seen_now ^ jnp.arange(block_last)]
+        ready = shifts_all_remake(lower, q_in)
+        return ready
+
     outputs = per_head(
         (
             lax.all_to_all(to_heads(queries), "head", split_axis=1, concat_axis=0, tiled=True),
-            lax.all_to_all(to_heads(key_rows), "head", split_axis=1, concat_axis=0, tiled=True),
+            draw_quarters(to_heads(key_rows), "head", 1, 0),
             lax.all_to_all(to_heads(value_rows), "head", split_axis=1, concat_axis=0, tiled=True),
             lax.all_to_all(to_heads(out_grad), "head", split_axis=1, concat_axis=0, tiled=True),
         )

time: 175 us -> 169 us (0.966)
  waiting for transfers between devices: 98.2 us -> 88.8 us
    ppermute x0 -> x3, waiting for transfers between devices: none -> 18.7 us  [draw_quarters(): jax.lax.ppermute(w2, net_axis, [(q, q ^ ii) for q in range(block_last)])]
    all_to_all x1, waiting for transfers between devices: 13.9 us -> 0.01 us  [shards(): lax.all_to_all(to_heads(value_rows), 'head', split_axis=1, concat_axis=0,...]
    all_to_all x1 -> x0, waiting for transfers between devices: 13.4 us -> none  [shards(): lax.all_to_all(to_heads(key_rows), 'head', split_axis=1, concat_axis=0, t...]
    all_to_all x1, waiting for transfers between devices: 12.1 us -> 0.01 us  [per_head(): lax.all_to_all(results[2], 'head', split_axis=0, concat_axis=1, tiled=True)]
    all_gather x1, waiting for transfers between devices: 10.9 us -> 0.01 us  [per_head(): lax.all_gather(grad_total[None], 'seq', axis=0, tiled=True)]
    all_gather x1, waiting for transfers between devices: 0.01 us -> 9.53 us  [per_head(): lax.all_gather(kv_total[None], 'seq', axis=0, tiled=True)]
    all_to_all x1, waiting for transfers between devices: 0.01 us -> 8.53 us  [per_head(): lax.all_to_all(results[0], 'head', split_axis=0, concat_axis=1, tiled=True)]
    all_to_all x1 -> x0, starting transfers between devices: 6.32 us -> none  [shards(): lax.all_to_all(to_heads(key_rows), 'head', split_axis=1, concat_axis=0, t...]
  transfers between devices with their start and end apart: 10 -> 12, of which waited for: 8 -> 7; matrix products, arithmetic and copies ran while one was open for 14% -> 15% of each run, Pallas kernels for 0% -> 0%
where the time goes in v1:
time: 169 us; the launch traced here: 168 us
  waiting for transfers between devices  88.8 us (53%)
  starting transfers between devices  33.5 us (20%)
  local copies, waits for them, and re-layouts  18.1 us (11%)
  between operations  14.4 us (9%)
  matrix products  9.29 us (5%)
  other arithmetic  3.91 us (2%)
    ppermute x3, waiting for transfers between devices, draw_quarters(): jax.lax.ppermute(w2, net_axis, [(q, q ^ ii) for q in range(block_last)])  18.7 us
    all_to_all x1, waiting for transfers between devices, shards(): lax.all_to_all(to_heads(out_grad), 'head', split_axis=1, concat_axis=0, t...  13.9 us
    all_to_all x1, waiting for transfers between devices, shards(): lax.all_to_all(to_heads(queries), 'head', split_axis=1, concat_axis=0, ti...  13.4 us
    all_to_all x1, waiting for transfers between devices, per_head(): lax.all_to_all(results[1], 'head', split_axis=0, concat_axis=1, tiled=True)  12.7 us
    all_to_all x1, waiting for transfers between devices, per_head(): lax.all_to_all(results[3], 'head', split_axis=0, concat_axis=1, tiled=True)  12.1 us
    all_gather x1, waiting for transfers between devices, per_head(): lax.all_gather(kv_total[None], 'seq', axis=0, tiled=True)  9.53 us
    all_to_all x1, waiting for transfers between devices, per_head(): lax.all_to_all(results[0], 'head', split_axis=0, concat_axis=1, tiled=True)  8.53 us
    all_to_all x1, starting transfers between devices, shards(): lax.all_to_all(to_heads(queries), 'head', split_axis=1, concat_axis=0, ti...  6.32 us
  transfers between devices with their start and end apart: 12, of which 7 were waited for; matrix products, arithmetic and copies ran while one was open for 15% of the time, Pallas kernels for 0%

profile of v1, /device:TPU:0, one launch (start us, length us, event | category | flops | bytes accessed | tf_op | source)
XLA Modules:
  0.0 168.0 jit_solution(13176079058529752644)
XLA Ops:
  7.2 1.2 copy.137
  9.4 6.3 %all-to-all-start = ((bf16[64,4,8,128]{3,0,2,1:T(8,128)(2,1)}), bf16[64,4,8,128]{3,0,2,1:T(8,128)(2,1)S(1)}, u32[]{:S(2)}, u32[]{:S(2)}) async-start(bf16[64,4,8,128]{3,0,2,1:T(8,128)(2,1)} %copy.91), calls=%async_computation | async-start | bytes 1048576 | tf_op jit(solution)/shard_map/all_to_all | solution.py:123
  16.8 13.4 %all-to-all-done = bf16[64,4,8,128]{3,0,2,1:T(8,128)(2,1)S(1)} async-done(((bf16[64,4,8,128]{3,0,2,1:T(8,128)(2,1)}), bf16[64,4,8,128]{3,0,2,1:T(8,128)(2,1)S(1)}, u32[]{:S(2)}, u32[]{:S(2)}) %all-to-all-start) | async-done | bytes 524320 | tf_op jit(solution)/shard_map/all_to_all | solution.py:123
  30.2 3.5 %all-to-all-start.3 = ((bf16[64,4,8,128]{3,0,2,1:T(8,128)(2,1)}), bf16[64,4,8,128]{3,0,2,1:T(8,128)(2,1)S(1)}, u32[]{:S(2)}, u32[]{:S(2)}) async-start(bf16[64,4,8,128]{3,0,2,1:T(8,128)(2,1)} %copy.103), calls=%async_computation.3 | async-start | bytes 1048576 | tf_op jit(solution)/shard_map/all_to_all | solution.py:126
  33.8 13.9 %all-to-all-done.3 = bf16[64,4,8,128]{3,0,2,1:T(8,128)(2,1)S(1)} async-done(((bf16[64,4,8,128]{3,0,2,1:T(8,128)(2,1)}), bf16[64,4,8,128]{3,0,2,1:T(8,128)(2,1)S(1)}, u32[]{:S(2)}, u32[]{:S(2)}) %all-to-all-start.3) | async-done | bytes 524320 | tf_op jit(solution)/shard_map/all_to_all | solution.py:126
  47.7 1.1 fusion.22
  49.9 3.5 %all-to-all-start.1 = ((bf16[64,4,8,128]{3,0,2,1:T(8,128)(2,1)}), bf16[64,4,8,128]{3,0,2,1:T(8,128)(2,1)S(1)}, u32[]{:S(2)}, u32[]{:S(2)}) async-start(bf16[64,4,8,128]{3,0,2,1:T(8,128)(2,1)} %copy.95), calls=%async_computation.1 | async-start | bytes 1048576 | tf_op jit(solution)/shard_map/all_to_all | solution.py:125
  53.7 2.9 %collective-permute-start.1 = (bf16[64,1,8,128]{3,2,0,1:T(8,128)(2,1)S(1)}, bf16[64,1,8,128]{3,2,0,1:T(8,128)(2,1)S(1)}, u32[]{:S(2)}, u32[]{:S(2)}) collective-permute-start(bf16[64,1,8,128]{3,2,0,1:T(8,128)(2,1)S(1)} %get-tuple-element.5), channel_id=1, source_target_pairs={{0,2},{1,3},{2,0},{3,1},{4,6},{5,7},{6,4},{7,5},{8,10},{9,11},{10,... | collective-permute-start | bytes 393224 | tf_op jit(solution)/shard_map/ppermute | solution.py:113
  56.6 1.5 collective-permute-start
  58.2 18.7 %collective-permute-done.1 = bf16[64,1,8,128]{3,2,0,1:T(8,128)(2,1)S(1)} collective-permute-done((bf16[64,1,8,128]{3,2,0,1:T(8,128)(2,1)S(1)}, bf16[64,1,8,128]{3,2,0,1:T(8,128)(2,1)S(1)}, u32[]{:S(2)}, u32[]{:S(2)}) %collective-permute-start.1) | collective-permute-done | bytes 131104 | tf_op jit(solution)/shard_map/ppermute | solution.py:113
  80.6 1.4 convolution_bitcast_fusion.1
  82.0 1.9 %multiply_reduce_fusion = bf16[8,128,128]{2,1,0:T(8,128)(2,1)S(1)} fusion(f32[4,8,128,128]{3,2,1,0:T(8,128)} %bitcast.150, f32[4]{0:T(128)S(1)} %compare_convert_fusion), kind=kLoop, calls=%fused_computation.3 | loop fusion | flops 917504 | bytes 2359312 | tf_op jit(solution)/shard_map/reduce_sum | solution.py:65
  84.3 1.1 copy.114
  85.4 4.1 %all-to-all-start.5 = ((bf16[256,1,8,128]{3,2,1,0:T(8,128)(2,1)}), bf16[256,1,8,128]{3,2,1,0:T(8,128)(2,1)}, u32[]{:S(2)}, u32[]{:S(2)}) async-start(bf16[256,1,8,128]{3,2,1,0:T(8,128)(2,1)} %copy.114), calls=%async_computation.5 | async-start | bytes 1048576 | tf_op jit(solution)/shard_map/all_to_all | solution.py:100
  89.6 2.7 %fusion.21 = f32[8,128,256]{1,2,0:T(8,128)} fusion(bf16[256,8,128]{0,2,1:T(8,128)(2,1)S(1)} %copy.98, bf16[8,256,256]{1,2,0:T(8,128)(2,1)} %copy-done), kind=kOutput, calls=%fused_computation.43 | convolution fusion | flops 134217728 | bytes 2621440 | tf_op jit(solution)/shard_map/bhts,bshd->bthd/dot_general | solution.py:79
  92.3 9.5 %all-gather.5.cloned.1.call-done = f32[32,128,128]{2,1,0:T(8,128)} async-done(((f32[8,128,128]{2,1,0:T(8,128)}), f32[32,128,128]{2,1,0:T(8,128)}) %all-gather.5.cloned.1.call-update) | async-done | bytes 2097168 | tf_op jit(solution)/shard_map/all_gather | solution.py:57
  101.8 1.9 %multiply_reduce_fusion.1 = bf16[8,128,128]{2,1,0:T(8,128)(2,1)S(1)} fusion(f32[4,8,128,128]{3,2,1,0:T(8,128)} %bitcast.151, f32[4]{0:T(128)S(1)} %compare_convert_fusion.1), kind=kLoop, calls=%fused_computation.5 | loop fusion | flops 917504 | bytes 2359312 | tf_op jit(solution)/shard_map/reduce_sum | solution.py:64
  105.5 4.6 %all-to-all-start.4 = ((bf16[256,1,8,128]{3,2,1,0:T(8,128)(2,1)}), bf16[256,1,8,128]{3,2,1,0:T(8,128)(2,1)}, u32[]{:S(2)}, u32[]{:S(2)}) async-start(bf16[256,1,8,128]{3,2,1,0:T(8,128)(2,1)} %copy.110), calls=%async_computation.4 | async-start | bytes 1048576 | tf_op jit(solution)/shard_map/all_to_all | solution.py:99
  111.3 1.1 copy.119
  112.4 12.7 %all-to-all-done.4 = bf16[256,1,8,128]{3,2,1,0:T(8,128)(2,1)} async-done(((bf16[256,1,8,128]{3,2,1,0:T(8,128)(2,1)}), bf16[256,1,8,128]{3,2,1,0:T(8,128)(2,1)}, u32[]{:S(2)}, u32[]{:S(2)}) %all-to-all-start.4) | async-done | bytes 524320 | tf_op jit(solution)/shard_map/all_to_all | solution.py:99
  125.1 3.5 %all-to-all-start.6 = ((bf16[256,1,8,128]{3,2,1,0:T(8,128)(2,1)}), bf16[256,1,8,128]{3,2,1,0:T(8,128)(2,1)S(1)}, u32[]{:S(2)}, u32[]{:S(2)}) async-start(bf16[256,1,8,128]{3,2,1,0:T(8,128)(2,1)} %copy.119), calls=%async_computation.6 | async-start | bytes 1048576 | tf_op jit(solution)/shard_map/all_to_all | solution.py:101
  130.5 12.1 %all-to-all-done.6 = bf16[256,1,8,128]{3,2,1,0:T(8,128)(2,1)S(1)} async-done(((bf16[256,1,8,128]{3,2,1,0:T(8,128)(2,1)}), bf16[256,1,8,128]{3,2,1,0:T(8,128)(2,1)S(1)}, u32[]{:S(2)}, u32[]{:S(2)}) %all-to-all-start.6) | async-done | bytes 524320 | tf_op jit(solution)/shard_map/all_to_all | solution.py:101
  142.6 3.5 %all-to-all-start.2 = ((bf16[256,1,8,128]{3,2,1,0:T(8,128)(2,1)}), bf16[256,1,8,128]{3,2,1,0:T(8,128)(2,1)S(1)}, u32[]{:S(2)}, u32[]{:S(2)}) async-start(bf16[256,1,8,128]{3,2,1,0:T(8,128)(2,1)} %copy.101), calls=%async_computation.2 | async-start | bytes 1048576 | tf_op jit(solution)/shard_map/all_to_all | solution.py:98
  151.5 8.5 %all-to-all-done.2 = bf16[256,1,8,128]{3,2,1,0:T(8,128)(2,1)S(1)} async-done(((bf16[256,1,8,128]{3,2,1,0:T(8,128)(2,1)}), bf16[256,1,8,128]{3,2,1,0:T(8,128)(2,1)S(1)}, u32[]{:S(2)}, u32[]{:S(2)}) %all-to-all-start.2) | async-done | bytes 524320 | tf_op jit(solution)/shard_map/all_to_all | solution.py:98
  (63 shorter events, 19.0 us)
Async XLA Ops:
  7.2 8.5 %copy-start.5 = (bf16[64,4096]{1,0:T(8,128)(2,1)S(1)}, bf16[64,4096]{1,0:T(8,128)(2,1)}, u32[]{:S(2)}) copy-start(bf16[64,4096]{1,0:T(8,128)(2,1)} %param.7) | copy-start | bytes 1572868
  9.4 20.8 %all-to-all-start = ((bf16[64,4,8,128]{3,0,2,1:T(8,128)(2,1)}), bf16[64,4,8,128]{3,0,2,1:T(8,128)(2,1)S(1)}, u32[]{:S(2)}, u32[]{:S(2)}) async-start(bf16[64,4,8,128]{3,0,2,1:T(8,128)(2,1)} %copy.91), calls=%async_computation | async-start | bytes 1048576 | tf_op jit(solution)/shard_map/all_to_all | solution.py:123
  30.2 17.4 %all-to-all-start.3 = ((bf16[64,4,8,128]{3,0,2,1:T(8,128)(2,1)}), bf16[64,4,8,128]{3,0,2,1:T(8,128)(2,1)S(1)}, u32[]{:S(2)}, u32[]{:S(2)}) async-start(bf16[64,4,8,128]{3,0,2,1:T(8,128)(2,1)} %copy.103), calls=%async_computation.3 | async-start | bytes 1048576 | tf_op jit(solution)/shard_map/all_to_all | solution.py:126
  33.7 48.3 %all-gather.7.cloned.1.call-start = ((), (), s32[]{:S(2)}) async-start(), calls=%async_computation.8 | async-start | bytes 2621440 | tf_op jit(solution)/shard_map/all_gather | solution.py:58
  33.7 15.1 %copy-start.6 = (bf16[64,4096]{1,0:T(8,128)(2,1)S(1)}, bf16[64,4096]{1,0:T(8,128)(2,1)}, u32[]{:S(2)}) copy-start(bf16[64,4096]{1,0:T(8,128)(2,1)} %param.6) | copy-start | bytes 1572868
  48.8 4.7 %copy-start.7 = (bf16[64,4096]{1,0:T(8,128)(2,1)S(1)}, bf16[64,4096]{1,0:T(8,128)(2,1)}, u32[]{:S(2)}) copy-start(bf16[64,4096]{1,0:T(8,128)(2,1)} %param.5) | copy-start | bytes 1572868
  49.9 28.0 %all-to-all-start.1 = ((bf16[64,4,8,128]{3,0,2,1:T(8,128)(2,1)}), bf16[64,4,8,128]{3,0,2,1:T(8,128)(2,1)S(1)}, u32[]{:S(2)}, u32[]{:S(2)}) async-start(bf16[64,4,8,128]{3,0,2,1:T(8,128)(2,1)} %copy.95), calls=%async_computation.1 | async-start | bytes 1048576 | tf_op jit(solution)/shard_map/all_to_all | solution.py:125
  53.4 48.4 %all-gather.5.cloned.1.call-start = ((), (), s32[]{:S(2)}) async-start(), calls=%async_computation.7 | async-start | bytes 2621440 | tf_op jit(solution)/shard_map/all_gather | solution.py:57
  53.7 23.1 %collective-permute-start.1 = (bf16[64,1,8,128]{3,2,0,1:T(8,128)(2,1)S(1)}, bf16[64,1,8,128]{3,2,0,1:T(8,128)(2,1)S(1)}, u32[]{:S(2)}, u32[]{:S(2)}) collective-permute-start(bf16[64,1,8,128]{3,2,0,1:T(8,128)(2,1)S(1)} %get-tuple-element.5), channel_id=1, source_target_pairs={{0,2},{1,3},{2,0},{3,1},{4,6},{5,7},{6,4},{7,5},{8,10},{9,11},{10,... | collective-permute-start | bytes 393224 | tf_op jit(solution)/shard_map/ppermute | solution.py:113
  56.6 20.3 %collective-permute-start = (bf16[64,1,8,128]{3,2,0,1:T(8,128)(2,1)S(1)}, bf16[64,1,8,128]{3,2,0,1:T(8,128)(2,1)S(1)}, u32[]{:S(2)}, u32[]{:S(2)}) collective-permute-start(bf16[64,1,8,128]{3,2,0,1:T(8,128)(2,1)S(1)} %get-tuple-element.6), channel_id=1, source_target_pairs={{0,1},{1,0},{2,3},{3,2},{4,5},{5,4},{6,7},{7,6},{8,9},{9,8},{10,11... | collective-permute-start | bytes 393224 | tf_op jit(solution)/shard_map/ppermute | solution.py:113
  58.1 18.8 %collective-permute-start.2 = (bf16[64,1,8,128]{3,2,0,1:T(8,128)(2,1)S(1)}, bf16[64,1,8,128]{3,2,0,1:T(8,128)(2,1)S(1)}, u32[]{:S(2)}, u32[]{:S(2)}) collective-permute-start(bf16[64,1,8,128]{3,2,0,1:T(8,128)(2,1)S(1)} %get-tuple-element.7), channel_id=1, source_target_pairs={{0,3},{1,2},{2,1},{3,0},{4,7},{5,6},{6,5},{7,4},{8,11},{9,10},{10,... | collective-permute-start | bytes 393224 | tf_op jit(solution)/shard_map/ppermute | solution.py:113
  79.6 1.0 copy-start
  82.0 1.9 %copy-start.2 = (f32[8,128,256]{1,2,0:T(8,128)S(1)}, f32[8,128,256]{1,2,0:T(8,128)}, u32[]{:S(2)}) copy-start(f32[8,128,256]{1,2,0:T(8,128)} %convolution_bitcast_fusion.1) | copy-start | bytes 3145732
  85.4 20.1 %all-to-all-start.5 = ((bf16[256,1,8,128]{3,2,1,0:T(8,128)(2,1)}), bf16[256,1,8,128]{3,2,1,0:T(8,128)(2,1)}, u32[]{:S(2)}, u32[]{:S(2)}) async-start(bf16[256,1,8,128]{3,2,1,0:T(8,128)(2,1)} %copy.114), calls=%async_computation.5 | async-start | bytes 1048576 | tf_op jit(solution)/shard_map/all_to_all | solution.py:100
  92.3 11.4 %copy-start.1 = (f32[8,128,256]{1,2,0:T(8,128)S(1)}, f32[8,128,256]{1,2,0:T(8,128)}, u32[]{:S(2)}) copy-start(f32[8,128,256]{1,2,0:T(8,128)} %fusion.21) | copy-start | bytes 3145732
  103.6 0.7 copy-start.3
  105.5 19.6 %all-to-all-start.4 = ((bf16[256,1,8,128]{3,2,1,0:T(8,128)(2,1)}), bf16[256,1,8,128]{3,2,1,0:T(8,128)(2,1)}, u32[]{:S(2)}, u32[]{:S(2)}) async-start(bf16[256,1,8,128]{3,2,1,0:T(8,128)(2,1)} %copy.110), calls=%async_computation.4 | async-start | bytes 1048576 | tf_op jit(solution)/shard_map/all_to_all | solution.py:99
  112.4 16.7 %copy-start.4 = (bf16[8,128,128]{2,1,0:T(8,128)(2,1)S(1)}, bf16[8,128,128]{2,1,0:T(8,128)(2,1)}, u32[]{:S(2)}) copy-start(bf16[8,128,128]{2,1,0:T(8,128)(2,1)} %copy-done.3) | copy-start | bytes 786436
  125.1 17.5 %all-to-all-start.6 = ((bf16[256,1,8,128]{3,2,1,0:T(8,128)(2,1)}), bf16[256,1,8,128]{3,2,1,0:T(8,128)(2,1)S(1)}, u32[]{:S(2)}, u32[]{:S(2)}) async-start(bf16[256,1,8,128]{3,2,1,0:T(8,128)(2,1)} %copy.119), calls=%async_computation.6 | async-start | bytes 1048576 | tf_op jit(solution)/shard_map/all_to_all | solution.py:101
  142.6 17.4 %all-to-all-start.2 = ((bf16[256,1,8,128]{3,2,1,0:T(8,128)(2,1)}), bf16[256,1,8,128]{3,2,1,0:T(8,128)(2,1)S(1)}, u32[]{:S(2)}, u32[]{:S(2)}) async-start(bf16[256,1,8,128]{3,2,1,0:T(8,128)(2,1)} %copy.101), calls=%async_computation.2 | async-start | bytes 1048576 | tf_op jit(solution)/shard_map/all_to_all | solution.py:98
Sparse Core Ops, SparseCore 0:
  49.0 21.6 all-gather.6
  79.2 22.5 all-gather.4
